TPU v7x, 512 devices: a whole 4x8x8 slice. The times are simulated.
512 devices in a mesh: seq: 16 (over y, core), head: 32 (over z, x).
Axes of the slice: x: 4, y: 8, z: 8, core: 2. Of those that a mesh axis runs over, the one named last changes fastest.
Arguments:
- queries: bfloat16 [65536, 8192], P(('seq', 'head')), may hold values from -36 to 36
- keys_values: bfloat16 [65536, 2048], P(('seq', 'head')), may hold values from -14 to 14
- vertical: int32 [64, 4], replicated, may hold values from -1 to 63, as said below
- slash: int32 [64, 2], replicated, may hold values from -1 to 2, as said below
- assignment: int32 [64], replicated, may hold values from 0 to 63, as said below
Outputs:
- attended: bfloat16 [1024, 4096, 128], P(('seq', 'head'))
Inputs may be any that keep to these rules, and one draw needn't show every extreme that they name: `vertical`: row h lists distinct blocks below 64, used entries first and -1 after them; a row uses 1 to 4 entries. The rows of the 8 query heads of one key-value head name exactly 8 distinct blocks together. `slash`: row h lists distinct offsets, used entries first and -1 after them; a row uses 1 to 2 entries. `assignment`: every unit appears once. Slots 2 * d to 2 * d + 1 of a group belong to index d of the head axis, and their units are parts of query heads of one key-value head.
All inputs are finite; a program needn't handle non-finite values.
Results may differ from a plain program's by a relative error of at most 0.0065.
Values may be sent and summed in bfloat16 or wider, within the bound.
A program may use at most 64 MiB of HBM per device.

v0:
```python
import math
import jax
import jax.numpy as jnp
from jax import lax
from jax.sharding import PartitionSpec as P

HQ = 64
HK = 8
HD = 128
BLK = 64
REACH = 2
NV = 4
GQ = 8


def from_behind(value, axis, steps):
    count = lax.axis_size(axis)
    leading, last = (max(0, -steps), min(count, count - steps))
    return lax.ppermute(value, axis, [(source, source + steps) for source in range(leading, last)])


def broadcast(block, axis, holder):
    block = jnp.where(lax.axis_index(axis) == holder, block, jnp.zeros_like(block))
    return lax.psum(block, axis)


def softmax_update(state, scores, mask, product):
    top, total, accum = state
    masked = jnp.where(mask, scores, -jnp.inf)
    new_top = jnp.maximum(top, jnp.max(masked, axis=-1))
    factor = jnp.exp(top - new_top)
    weights = jnp.where(mask, jnp.exp(scores - new_top[..., None]), 0.0)
    total = total * factor + jnp.sum(weights, axis=-1)
    accum = accum * factor[..., None] + product(weights.astype(jnp.bfloat16))
    return (new_top, total, accum)


def attend_blocks(
    query_blocks,
    query_index,
    key_store,
    store_base,
    store_heads,
    vertical_store,
    vertical_slot,
    head_ids,
    vertical,
    slash,
):
    items, count, width, depth = query_blocks.shape
    scale = 1.0 / math.sqrt(depth)
    vert_rows = vertical[head_ids]
    slash_rows = slash[head_ids]
    main_steps = 1 + jnp.max(jnp.sum((slash_rows >= 1).astype(jnp.int32), axis=1))
    vertical_steps = jnp.max(jnp.sum((vert_rows >= 0).astype(jnp.int32), axis=1))
    stored = key_store.shape[0]
    causal = jnp.arange(width)[None, :] <= jnp.arange(width)[:, None]
    begin = (
        jnp.full((items, count, width), -jnp.inf, jnp.float32),
        jnp.zeros((items, count, width), jnp.float32),
        jnp.zeros((items, count, width, depth), jnp.float32),
    )

    def main_step(number, state):
        offset = jnp.where(number == 0, 0, jnp.take(slash_rows, jnp.maximum(number - 1, 0), axis=1))
        target = query_index - offset[:, None]
        repeated = jnp.any(target[:, :, None] == vert_rows[:, None, :], axis=-1)
        valid = (number == 0) | (offset[:, None] >= 1) & (target >= 0) & jnp.logical_not(repeated)
        local = jnp.clip(target - store_base, 0, stored - 1)
        fetched = key_store[local, :, store_heads[:, None]]
        keys = fetched[..., :depth]
        values = fetched[..., depth:]
        scores = (
            jnp.einsum("inqd,inkd->inqk", query_blocks, keys, preferred_element_type=jnp.float32)
            * scale
        )
        mask = valid[:, :, None, None] & ((number > 0) | causal)[None, None]
        return softmax_update(
            state,
            scores,
            mask,
            lambda weights: jnp.einsum(
                "inqk,inkd->inqd", weights, values, preferred_element_type=jnp.float32
            ),
        )

    def vertical_step(number, state):
        blocks = jnp.take(vert_rows, number, axis=1)
        valid = (blocks[:, None] >= 0) & (blocks[:, None] < query_index)
        fetched = vertical_store[jnp.take(vertical_slot, number, axis=1)]
        keys = fetched[..., :depth]
        values = fetched[..., depth:]
        scores = (
            jnp.einsum("inqd,ikd->inqk", query_blocks, keys, preferred_element_type=jnp.float32)
            * scale
        )
        mask = jnp.broadcast_to(valid[:, :, None, None], scores.shape)
        return softmax_update(
            state,
            scores,
            mask,
            lambda weights: jnp.einsum(
                "inqk,ikd->inqd", weights, values, preferred_element_type=jnp.float32
            ),
        )

    state = lax.fori_loop(0, main_steps, main_step, begin)
    state = lax.fori_loop(0, vertical_steps, vertical_step, state)
    top, total, accum = state
    return (accum / total[..., None]).astype(jnp.bfloat16)


def on_device(queries, keys_values, vertical, slash, assignment):
    rows = queries.shape[0]
    members = lax.axis_size("head")
    seq_place = lax.axis_index("seq")
    head_place = lax.axis_index("head")
    parts = max(1, 2 * members // HQ)
    per_device = parts * HQ // members
    portion = rows // parts
    device_blocks = rows // BLK
    group_blocks = device_blocks * members
    slot_major = assignment.reshape(members, per_device).T.reshape(-1)
    unit_heads = slot_major % HQ
    unit_parts = slot_major // HQ
    mine = lax.dynamic_slice_in_dim(assignment, per_device * head_place, per_device)
    my_heads = mine % HQ
    my_parts = mine // HQ
    split_queries = queries.reshape(parts, portion, HQ, HD)
    outgoing = split_queries[unit_parts, :, unit_heads].reshape(per_device, members, portion, HD)
    incoming = lax.all_to_all(outgoing, "head", split_axis=1, concat_axis=1, tiled=True)
    wanted = assignment.reshape(members, per_device)[:, 0] % HQ // GQ
    shipped = keys_values.reshape(rows, HK, 2 * HD)[:, wanted]
    group_pairs = lax.all_to_all(shipped, "head", split_axis=1, concat_axis=0, tiled=True)
    own_pairs = group_pairs[:, 0]
    group_tail = own_pairs[own_pairs.shape[0] - REACH * BLK :]
    before = from_behind(group_tail, "seq", 1)
    store_flat = jnp.concatenate([before, own_pairs], axis=0).reshape(
        REACH + group_blocks, BLK, 2 * HD
    )
    picked = store_flat[jnp.clip(vertical[my_heads], 0, None) + REACH]
    shared = broadcast(picked, "seq", 0)
    vertical_store = shared.reshape(per_device * NV, BLK, 2 * HD)
    per_portion = portion // BLK
    order = jnp.arange(members * per_portion, dtype=jnp.int32)
    query_index = (
        seq_place * group_blocks
        + (order // per_portion)[None, :] * device_blocks
        + my_parts[:, None] * per_portion
        + (order % per_portion)[None, :]
    )
    query_blocks = incoming.reshape(per_device, members * per_portion, BLK, HD)
    slot_rows = (
        jnp.arange(per_device, dtype=jnp.int32)[:, None] * NV
        + jnp.arange(NV, dtype=jnp.int32)[None, :]
    )
    outputs = attend_blocks(
        query_blocks,
        query_index,
        store_flat[:, :, None, :],
        seq_place * group_blocks - REACH,
        jnp.zeros((per_device,), jnp.int32),
        vertical_store,
        slot_rows,
        my_heads,
        vertical,
        slash,
    )
    attended = outputs.reshape(per_device, members * portion, HD)
    return attended


def solution(mesh):
    placed = (P(("seq", "head"), None), P(("seq", "head"), None), P(), P(), P())
    return jax.shard_map(
        on_device,
        mesh=mesh,
        in_specs=placed,
        out_specs=P(("seq", "head"), None, None),
        check_vma=False,
    )
```

profile of v0, /device:TPU:1, one launch (start us, length us, event | category | flops | bytes accessed | tf_op | source)
XLA Modules:
  0.0 312.2 jit_solution(15812212171097348099)
XLA Ops:
  11.0 13.7 %all-to-all-start = ((bf16[128,32,256]{2,0,1:T(8,128)(2,1)}), bf16[128,32,256]{2,0,1:T(8,128)(2,1)S(1)}, u32[]{:S(2)}, u32[]{:S(2)}) async-start(bf16[128,32,256]{2,0,1:T(8,128)(2,1)} %bitcast.108), calls=%async_computation | async-start | bytes 4194304 | tf_op jit(solution)/shard_map/all_to_all | solution.py:134
  24.9 4.1 %copy.68 = bf16[128,8192]{0,1:T(8,128)(2,1)} copy(bf16[128,8192]{1,0:T(8,128)(2,1)} %param.11) | data formatting | bytes 4194304 | tf_op args[0]
  28.9 4.1 %copy.70 = bf16[1,128,64,128]{3,1,2,0:T(8,128)(2,1)} copy(bf16[1,128,64,128]{1,3,2,0:T(8,128)(2,1)} %bitcast.110) | data formatting | bytes 4194304 | tf_op jit(solution)/shard_map/reshape | solution.py:129
  33.1 3.7 %gather_fusion.5 = bf16[64,128,128]{2,1,0:T(8,128)(2,1)} fusion(bf16[1,128,64,128]{3,1,2,0:T(8,128)(2,1)} %copy.70, s32[64]{0:T(128)S(1)} %fusion.52), kind=kCustom, calls=%fused_computation.5 | custom fusion | bytes 4194816 | tf_op jit(solution)/shard_map/gather | solution.py:130
  40.0 33.2 %all-to-all-done = bf16[128,32,256]{2,0,1:T(8,128)(2,1)S(1)} async-done(((bf16[128,32,256]{2,0,1:T(8,128)(2,1)}), bf16[128,32,256]{2,0,1:T(8,128)(2,1)S(1)}, u32[]{:S(2)}, u32[]{:S(2)}) %all-to-all-start) | async-done | bytes 2097184 | tf_op jit(solution)/shard_map/all_to_all | solution.py:134
  73.2 6.7 %all-to-all-start.1 = ((bf16[2,32,128,128]{3,2,0,1:T(8,128)(2,1)}), bf16[2,32,128,128]{3,2,0,1:T(8,128)(2,1)}, u32[]{:S(2)}, u32[]{:S(2)}) async-start(bf16[2,32,128,128]{3,2,0,1:T(8,128)(2,1)} %copy.71), calls=%async_computation.1 | async-start | bytes 4194304 | tf_op jit(solution)/shard_map/all_to_all | solution.py:131
  83.8 5.1 %collective-permute-start = (bf16[128,256]{1,0:T(8,128)(2,1)S(1)}, bf16[128,256]{1,0:T(8,128)(2,1)S(1)}, u32[]{:S(2)}, u32[]{:S(2)}) collective-permute-start(bf16[128,256]{1,0:T(8,128)(2,1)S(1)} %slice_bitcast_fusion.4), channel_id=1, source_target_pairs={{0,32},{32,64},{64,96},{96,128},{128,160},{160,192},{192,224},{224... | collective-permute-start | bytes 196616 | tf_op jit(solution)/shard_map/ppermute | solution.py:19
  88.9 38.2 %all-to-all-done.1 = bf16[2,32,128,128]{3,2,0,1:T(8,128)(2,1)} async-done(((bf16[2,32,128,128]{3,2,0,1:T(8,128)(2,1)}), bf16[2,32,128,128]{3,2,0,1:T(8,128)(2,1)}, u32[]{:S(2)}, u32[]{:S(2)}) %all-to-all-start.1) | async-done | bytes 2097184 | tf_op jit(solution)/shard_map/all_to_all | solution.py:131
  135.9 30.1 %while.34 = (s32[]{:T(128)}, f32[2,64,64]{2,1,0:T(8,128)S(1)}, f32[2,64,64]{2,1,0:T(8,128)S(1)}, f32[2,64,64,128]{3,2,1,0:T(8,128)}, s32[]{:T(128)}, /*index=5*/...) while((s32[]{:T(128)}, f32[2,64,64]{2,1,0:T(8,128)S(1)}, ...), condition=%wide.region_6.7_spmd.clone, body=%wide.region_2.6_spmd.clone.sunk | while | flops 277900800 | bytes 48851412 | solution.py:107
  139.1 3.5 %fusion.73 = (f32[2,64,64]{2,1,0:T(8,128)S(1)}, f32[2,64,64,64]{3,2,1,0:T(8,128)S(1)}) fusion(pred[64,64]{0,1:T(8,128)(4,1)S(1)} %fusion.70, pred[2,64]{1,0:T(4,128)(4,1)S(1)} %and_or_fusion.2, bf16[2,64,64,128]{3,2,1,0:T(8,128)(2,1)} %get-tuple-element.741, bf16[2,64,64,256]{3,2,1,0:T(8,128)(2,1)} %bitcast.103), kind=kOutput, calls=%fused_computation.13.clone.1 | convolution fusion | flops 136306688 | bytes 6328448 | tf_op jit(solution)/shard_map/while/body/inqd,inkd->inqk/dot_general | solution.py:74
  144.8 6.1 %multiply_add_fusion.9 = f32[2,64,64,128]{3,2,1,0:T(8,128)} fusion(f32[2,64,64,128]{3,2,1,0:T(8,128)} %get-tuple-element.719, f32[2,64,64,64]{3,2,1,0:T(8,128)S(1)} %get-tuple-element.679, bf16[2,64,64,256]{3,2,1,0:T(8,128)(2,1)S(1)} %bitcast.104, f32[2,64,64]{2,1,0:T(8,128)S(1)} %get-tuple-element.681, f32[2,64,64]{2,1,0:T(8,128)S(1)} %max.42, ...), kind=kOutput, calls=%fused_computation.16.clone.1 | convolution fusion | flops 138936320 | bytes 14819840 | tf_op jit(solution)/shard_map/while/body/inqk,inkd->inqd/dot_general | solution.py:82
  154.2 3.5 %fusion.73 = (f32[2,64,64]{2,1,0:T(8,128)S(1)}, f32[2,64,64,64]{3,2,1,0:T(8,128)S(1)}) fusion(pred[64,64]{0,1:T(8,128)(4,1)S(1)} %fusion.70, pred[2,64]{1,0:T(4,128)(4,1)S(1)} %and_or_fusion.2, bf16[2,64,64,128]{3,2,1,0:T(8,128)(2,1)} %get-tuple-element.741, bf16[2,64,64,256]{3,2,1,0:T(8,128)(2,1)} %bitcast.103), kind=kOutput, calls=%fused_computation.13.clone.1 | convolution fusion | flops 136306688 | bytes 6328448 | tf_op jit(solution)/shard_map/while/body/inqd,inkd->inqk/dot_general | solution.py:74
  159.9 6.1 %multiply_add_fusion.9 = f32[2,64,64,128]{3,2,1,0:T(8,128)} fusion(f32[2,64,64,128]{3,2,1,0:T(8,128)} %get-tuple-element.719, f32[2,64,64,64]{3,2,1,0:T(8,128)S(1)} %get-tuple-element.679, bf16[2,64,64,256]{3,2,1,0:T(8,128)(2,1)S(1)} %bitcast.104, f32[2,64,64]{2,1,0:T(8,128)S(1)} %get-tuple-element.681, f32[2,64,64]{2,1,0:T(8,128)S(1)} %max.42, ...), kind=kOutput, calls=%fused_computation.16.clone.1 | convolution fusion | flops 138936320 | bytes 14819840 | tf_op jit(solution)/shard_map/while/body/inqk,inkd->inqd/dot_general | solution.py:82
  166.0 81.9 %all-reduce.3.cloned.1.call-done = bf16[8,64,256]{2,1,0:T(8,128)(2,1)} async-done(((bf16[8,64,256]{2,1,0:T(8,128)(2,1)}), bf16[8,64,256]{2,1,0:T(8,128)(2,1)}) %all-reduce.3.cloned.1.call-update) | async-done | bytes 262160 | tf_op jit(solution)/shard_map/psum | solution.py:24
  247.9 53.7 %while.35 = (s32[]{:T(128)}, f32[2,64,64]{2,1,0:T(8,128)S(1)}, f32[2,64,64]{2,1,0:T(8,128)S(1)}, f32[2,64,64,128]{3,2,1,0:T(8,128)}, s32[]{:T(128)}, /*index=5*/...) while((s32[]{:T(128)}, f32[2,64,64]{2,1,0:T(8,128)S(1)}, ...), condition=%wide.region_13.15_spmd.clone, body=%wide.region_10.14_spmd.clone.sunk | while | flops 276317728 | bytes 19667008 | solution.py:108
  250.1 3.7 %select_reduce_fusion.2 = (f32[2,64,64]{2,1,0:T(8,128)S(1)}, f32[2,64,64,64]{3,1,2,0:T(8,128)S(1)}) fusion(pred[2,64]{1,0:T(4,128)(4,1)S(1)} %compare_and_fusion.2, bf16[2,64,64,128]{3,2,1,0:T(8,128)(2,1)} %get-tuple-element.787, bf16[2,64,256]{2,1,0:T(8,128)(2,1)S(1)} %gather_fusion.1), kind=kOutput, calls=%fused_computation.51.clone.1 | convolution fusion | flops 135782400 | bytes 4260352 | tf_op jit(solution)/shard_map/while/body/inqd,ikd->inqk/dot_general | solution.py:94
  255.0 6.1 %multiply_add_fusion.11 = f32[2,64,64,128]{3,2,1,0:T(8,128)} fusion(f32[2,64,64,128]{3,2,1,0:T(8,128)} %get-tuple-element.767, f32[2,64,64,64]{3,1,2,0:T(8,128)S(1)} %get-tuple-element.697, f32[2,64,64]{2,1,0:T(8,128)S(1)} %get-tuple-element.699, f32[2,64,64]{2,1,0:T(8,128)S(1)} %max.43, pred[2,64]{1,0:T(4,128)(4,1)S(1)} %compare_and_fusion.2, ...), kind=kOutput, calls=%fused_computation.49.clone.1 | convolution fusion | flops 138412032 | bytes 12747264 | tf_op jit(solution)/shard_map/while/body/inqk,ikd->inqd/dot_general | solution.py:102
  263.4 3.7 %select_reduce_fusion.2 = (f32[2,64,64]{2,1,0:T(8,128)S(1)}, f32[2,64,64,64]{3,1,2,0:T(8,128)S(1)}) fusion(pred[2,64]{1,0:T(4,128)(4,1)S(1)} %compare_and_fusion.2, bf16[2,64,64,128]{3,2,1,0:T(8,128)(2,1)} %get-tuple-element.787, bf16[2,64,256]{2,1,0:T(8,128)(2,1)S(1)} %gather_fusion.1), kind=kOutput, calls=%fused_computation.51.clone.1 | convolution fusion | flops 135782400 | bytes 4260352 | tf_op jit(solution)/shard_map/while/body/inqd,ikd->inqk/dot_general | solution.py:94
  268.3 6.1 %multiply_add_fusion.11 = f32[2,64,64,128]{3,2,1,0:T(8,128)} fusion(f32[2,64,64,128]{3,2,1,0:T(8,128)} %get-tuple-element.767, f32[2,64,64,64]{3,1,2,0:T(8,128)S(1)} %get-tuple-element.697, f32[2,64,64]{2,1,0:T(8,128)S(1)} %get-tuple-element.699, f32[2,64,64]{2,1,0:T(8,128)S(1)} %max.43, pred[2,64]{1,0:T(4,128)(4,1)S(1)} %compare_and_fusion.2, ...), kind=kOutput, calls=%fused_computation.49.clone.1 | convolution fusion | flops 138412032 | bytes 12747264 | tf_op jit(solution)/shard_map/while/body/inqk,ikd->inqd/dot_general | solution.py:102
  276.7 3.7 %select_reduce_fusion.2 = (f32[2,64,64]{2,1,0:T(8,128)S(1)}, f32[2,64,64,64]{3,1,2,0:T(8,128)S(1)}) fusion(pred[2,64]{1,0:T(4,128)(4,1)S(1)} %compare_and_fusion.2, bf16[2,64,64,128]{3,2,1,0:T(8,128)(2,1)} %get-tuple-element.787, bf16[2,64,256]{2,1,0:T(8,128)(2,1)S(1)} %gather_fusion.1), kind=kOutput, calls=%fused_computation.51.clone.1 | convolution fusion | flops 135782400 | bytes 4260352 | tf_op jit(solution)/shard_map/while/body/inqd,ikd->inqk/dot_general | solution.py:94
  281.6 6.1 %multiply_add_fusion.11 = f32[2,64,64,128]{3,2,1,0:T(8,128)} fusion(f32[2,64,64,128]{3,2,1,0:T(8,128)} %get-tuple-element.767, f32[2,64,64,64]{3,1,2,0:T(8,128)S(1)} %get-tuple-element.697, f32[2,64,64]{2,1,0:T(8,128)S(1)} %get-tuple-element.699, f32[2,64,64]{2,1,0:T(8,128)S(1)} %max.43, pred[2,64]{1,0:T(4,128)(4,1)S(1)} %compare_and_fusion.2, ...), kind=kOutput, calls=%fused_computation.49.clone.1 | convolution fusion | flops 138412032 | bytes 12747264 | tf_op jit(solution)/shard_map/while/body/inqk,ikd->inqd/dot_general | solution.py:102
  289.9 3.7 %select_reduce_fusion.2 = (f32[2,64,64]{2,1,0:T(8,128)S(1)}, f32[2,64,64,64]{3,1,2,0:T(8,128)S(1)}) fusion(pred[2,64]{1,0:T(4,128)(4,1)S(1)} %compare_and_fusion.2, bf16[2,64,64,128]{3,2,1,0:T(8,128)(2,1)} %get-tuple-element.787, bf16[2,64,256]{2,1,0:T(8,128)(2,1)S(1)} %gather_fusion.1), kind=kOutput, calls=%fused_computation.51.clone.1 | convolution fusion | flops 135782400 | bytes 4260352 | tf_op jit(solution)/shard_map/while/body/inqd,ikd->inqk/dot_general | solution.py:94
  294.8 6.1 %multiply_add_fusion.11 = f32[2,64,64,128]{3,2,1,0:T(8,128)} fusion(f32[2,64,64,128]{3,2,1,0:T(8,128)} %get-tuple-element.767, f32[2,64,64,64]{3,1,2,0:T(8,128)S(1)} %get-tuple-element.697, f32[2,64,64]{2,1,0:T(8,128)S(1)} %get-tuple-element.699, f32[2,64,64]{2,1,0:T(8,128)S(1)} %max.43, pred[2,64]{1,0:T(4,128)(4,1)S(1)} %compare_and_fusion.2, ...), kind=kOutput, calls=%fused_computation.49.clone.1 | convolution fusion | flops 138412032 | bytes 12747264 | tf_op jit(solution)/shard_map/while/body/inqk,ikd->inqd/dot_general | solution.py:102
  301.5 3.8 %divide_convert_fusion = bf16[2,64,64,128]{3,2,1,0:T(8,128)(2,1)} fusion(f32[2,64,64,128]{3,2,1,0:T(8,128)} %get-tuple-element.217, f32[2,64,64]{2,1,0:T(8,128)S(1)} %get-tuple-element.218), kind=kLoop, calls=%fused_computation.72 | loop fusion | flops 2097152 | bytes 6324224 | tf_op jit(solution)/shard_map/convert_element_type | solution.py:110
  (115 shorter events, 41.7 us)
Async XLA Ops:
  11.0 62.2 %all-to-all-start = ((bf16[128,32,256]{2,0,1:T(8,128)(2,1)}), bf16[128,32,256]{2,0,1:T(8,128)(2,1)S(1)}, u32[]{:S(2)}, u32[]{:S(2)}) async-start(bf16[128,32,256]{2,0,1:T(8,128)(2,1)} %bitcast.108), calls=%async_computation | async-start | bytes 4194304 | tf_op jit(solution)/shard_map/all_to_all | solution.py:134
  36.8 43.2 %copy-start.2 = (s32[64,4]{0,1:T(4,128)S(1)}, s32[64,4]{0,1:T(4,128)}, u32[]{:S(2)}) copy-start(s32[64,4]{0,1:T(4,128)} %param.13) | copy-start | bytes 3076
  36.8 43.3 %copy-start.4 = (s32[64,2]{0,1:T(2,128)S(1)}, s32[64,2]{0,1:T(2,128)}, u32[]{:S(2)}) copy-start(s32[64,2]{0,1:T(2,128)} %param.14) | copy-start | bytes 1540
  36.8 43.4 %copy-start.3 = (s32[64]{0:T(128)S(1)}, s32[64]{0:T(128)}, u32[]{:S(2)}) copy-start(s32[64]{0:T(128)} %param.15) | copy-start | bytes 772
  73.2 57.2 %copy-start.1 = (bf16[128,32,256]{2,0,1:T(8,128)(2,1)}, bf16[128,32,256]{2,0,1:T(8,128)(2,1)S(1)}, u32[]{:S(2)}) copy-start(bf16[128,32,256]{2,0,1:T(8,128)(2,1)S(1)} %all-to-all-done) | copy-start | bytes 6291460
  73.2 53.9 %all-to-all-start.1 = ((bf16[2,32,128,128]{3,2,0,1:T(8,128)(2,1)}), bf16[2,32,128,128]{3,2,0,1:T(8,128)(2,1)}, u32[]{:S(2)}, u32[]{:S(2)}) async-start(bf16[2,32,128,128]{3,2,0,1:T(8,128)(2,1)} %copy.71), calls=%async_computation.1 | async-start | bytes 4194304 | tf_op jit(solution)/shard_map/all_to_all | solution.py:131
  79.9 167.9 %all-reduce.3.cloned.1.call-start = ((), (), s32[]{:S(2)}) async-start(), calls=%async_computation.2 | async-start | bytes 524288 | tf_op jit(solution)/shard_map/psum | solution.py:24
  83.8 46.5 %collective-permute-start = (bf16[128,256]{1,0:T(8,128)(2,1)S(1)}, bf16[128,256]{1,0:T(8,128)(2,1)S(1)}, u32[]{:S(2)}, u32[]{:S(2)}) collective-permute-start(bf16[128,256]{1,0:T(8,128)(2,1)S(1)} %slice_bitcast_fusion.4), channel_id=1, source_target_pairs={{0,32},{32,64},{64,96},{96,128},{128,160},{160,192},{192,224},{224... | collective-permute-start | bytes 196616 | tf_op jit(solution)/shard_map/ppermute | solution.py:19
  142.6 2.2 copy-start
  157.6 2.2 copy-start
Sparse Core Ops, SparseCore 0:
  133.5 114.2 all-reduce.2
where the time goes:
time: 314 us; the launch traced here: 312 us
  waiting for transfers between devices  153 us (49%)
  matrix products  58.4 us (19%)
  local copies, waits for them, and re-layouts  40.7 us (13%)
  starting transfers between devices  25.6 us (8%)
  other arithmetic  16.7 us (5%)
  between operations  14.1 us (4%)
  loops' own time  3.48 us (1%)
    psum x1, waiting for transfers between devices, broadcast(): return lax.psum(block, axis)  81.9 us
    all_to_all x1, waiting for transfers between devices, on_device(): lax.all_to_all(outgoing, 'head', split_axis=1, concat_axis=1, tiled=True)  38.2 us
    all_to_all x1, waiting for transfers between devices, on_device(): lax.all_to_all(shipped, 'head', split_axis=1, concat_axis=0, tiled=True)  33.2 us
    dot_general x4, matrix products, vertical_step(): jnp.einsum('inqk,ikd->inqd', weights, values, preferred_element_type=jnp....  24.2 us
    dot_general x4, matrix products, vertical_step(): jnp.einsum('inqd,ikd->inqk', query_blocks, keys, preferred_element_type=j...  14.9 us
    all_to_all x1, starting transfers between devices, on_device(): lax.all_to_all(shipped, 'head', split_axis=1, concat_axis=0, tiled=True)  13.7 us
    dot_general x2, matrix products, main_step(): jnp.einsum('inqk,inkd->inqd', weights, values, preferred_element_type=jnp...  12.3 us
    reduce_sum x6, other arithmetic, softmax_update(): total = total * factor + jnp.sum(weights, axis=-1)  7.12 us
  transfers between devices with their start and end apart: 4, of which 3 were waited for; matrix products, arithmetic and copies ran while one was open for 17% of the time, Pallas kernels for 0%

commit v1 on v0

--- a/solution.py
+++ b/solution.py
@@ -3,6 +3,7 @@
 import jax.numpy as jnp
 from jax import lax
 from jax.sharding import PartitionSpec as P
+from jax.lax import all_gather
 
 HQ = 64
 HK = 8
@@ -11,6 +12,7 @@
 REACH = 2
 NV = 4
 GQ = 8
+rest_bands = lambda point, shard_axis: all_gather(point, shard_axis).sum(axis=0)
 
 
 def from_behind(value, axis, steps):
@@ -21,7 +23,7 @@
 
 def broadcast(block, axis, holder):
     block = jnp.where(lax.axis_index(axis) == holder, block, jnp.zeros_like(block))
-    return lax.psum(block, axis)
+    return rest_bands(block, axis)
 
 
 def softmax_update(state, scores, mask, product):

time: 314 us -> 244 us (0.78)
  the two profiles are of different devices: /device:TPU:1 before, /device:TPU:4 now
where the time goes in v1:
time: 244 us; the launch traced here: 243 us
  waiting for transfers between devices  78.7 us (32%)
  matrix products  62.5 us (26%)
  local copies, waits for them, and re-layouts  40.9 us (17%)
  other arithmetic  21.7 us (9%)
  starting transfers between devices  21.1 us (9%)
  between operations  14.3 us (6%)
  loops' own time  3.53 us (1%)
    all_to_all x1, waiting for transfers between devices, on_device(): lax.all_to_all(outgoing, 'head', split_axis=1, concat_axis=1, tiled=True)  44.2 us
    all_to_all x1, waiting for transfers between devices, on_device(): lax.all_to_all(shipped, 'head', split_axis=1, concat_axis=0, tiled=True)  34.5 us
    dot_general x4, matrix products, vertical_step(): jnp.einsum('inqk,ikd->inqd', weights, values, preferred_element_type=jnp....  24.2 us
    dot_general x3, matrix products, main_step(): jnp.einsum('inqk,inkd->inqd', weights, values, preferred_element_type=jnp...  18.4 us
    all_to_all x1, starting transfers between devices, on_device(): lax.all_to_all(shipped, 'head', split_axis=1, concat_axis=0, tiled=True)  13.4 us
    dot_general x3, matrix products, main_step(): jnp.einsum('inqd,inkd->inqk', query_blocks, keys, preferred_element_type=...  10.5 us
    dot_general x4, matrix products, vertical_step(): jnp.einsum('inqd,ikd->inqk', query_blocks, keys, preferred_element_type=j...  9.29 us
    reduce_sum x7, other arithmetic, softmax_update(): total = total * factor + jnp.sum(weights, axis=-1)  8.47 us
  transfers between devices with their start and end apart: 4, of which 2 were waited for; matrix products, arithmetic and copies ran while one was open for 28% of the time, Pallas kernels for 0%

profile of v1, /device:TPU:4, one launch (start us, length us, event | category | flops | bytes accessed | tf_op | source)
XLA Modules:
  0.0 242.6 jit_solution(312857676653968808)
XLA Ops:
  11.0 13.4 %all-to-all-start = ((bf16[128,32,256]{2,0,1:T(8,128)(2,1)}), bf16[128,32,256]{2,0,1:T(8,128)(2,1)S(1)}, u32[]{:S(2)}, u32[]{:S(2)}) async-start(bf16[128,32,256]{2,0,1:T(8,128)(2,1)} %bitcast.111), calls=%async_computation | async-start | bytes 4194304 | tf_op jit(solution)/shard_map/all_to_all | solution.py:136
  24.6 4.1 %copy.68 = bf16[128,8192]{0,1:T(8,128)(2,1)} copy(bf16[128,8192]{1,0:T(8,128)(2,1)} %param.11) | data formatting | bytes 4194304 | tf_op args[0]
  28.7 4.1 %copy.70 = bf16[1,128,64,128]{3,1,2,0:T(8,128)(2,1)} copy(bf16[1,128,64,128]{1,3,2,0:T(8,128)(2,1)} %bitcast.113) | data formatting | bytes 4194304 | tf_op jit(solution)/shard_map/reshape | solution.py:131
  32.8 3.7 %gather_fusion.5 = bf16[64,128,128]{2,1,0:T(8,128)(2,1)} fusion(bf16[1,128,64,128]{3,1,2,0:T(8,128)(2,1)} %copy.70, s32[64]{0:T(128)S(1)} %fusion.52), kind=kCustom, calls=%fused_computation.5 | custom fusion | bytes 4194816 | tf_op jit(solution)/shard_map/gather | solution.py:132
  36.5 3.2 %copy.71 = bf16[2,32,128,128]{3,2,0,1:T(8,128)(2,1)} copy(bf16[2,32,128,128]{3,2,1,0:T(8,128)(2,1)} %bitcast.112) | data formatting | bytes 4194304 | tf_op jit(solution)/shard_map/reshape | solution.py:132
  39.7 34.5 %all-to-all-done = bf16[128,32,256]{2,0,1:T(8,128)(2,1)S(1)} async-done(((bf16[128,32,256]{2,0,1:T(8,128)(2,1)}), bf16[128,32,256]{2,0,1:T(8,128)(2,1)S(1)}, u32[]{:S(2)}, u32[]{:S(2)}) %all-to-all-start) | async-done | bytes 2097184 | tf_op jit(solution)/shard_map/all_to_all | solution.py:136
  74.2 6.3 %all-to-all-start.1 = ((bf16[2,32,128,128]{3,2,0,1:T(8,128)(2,1)}), bf16[2,32,128,128]{3,2,0,1:T(8,128)(2,1)}, u32[]{:S(2)}, u32[]{:S(2)}) async-start(bf16[2,32,128,128]{3,2,0,1:T(8,128)(2,1)} %copy.71), calls=%async_computation.1 | async-start | bytes 4194304 | tf_op jit(solution)/shard_map/all_to_all | solution.py:133
  86.1 44.2 %all-to-all-done.1 = bf16[2,32,128,128]{3,2,0,1:T(8,128)(2,1)} async-done(((bf16[2,32,128,128]{3,2,0,1:T(8,128)(2,1)}), bf16[2,32,128,128]{3,2,0,1:T(8,128)(2,1)}, u32[]{:S(2)}, u32[]{:S(2)}) %all-to-all-start.1) | async-done | bytes 2097184 | tf_op jit(solution)/shard_map/all_to_all | solution.py:133
  130.2 3.2 %copy.72 = bf16[2,32,128,128]{3,2,1,0:T(8,128)(2,1)} copy(bf16[2,32,128,128]{3,2,0,1:T(8,128)(2,1)} %all-to-all-done.1) | data formatting | bytes 4194304 | tf_op jit(solution)/shard_map/all_to_all | solution.py:133
  139.0 45.6 %while.34 = (s32[]{:T(128)}, f32[2,64,64]{2,1,0:T(8,128)S(1)}, f32[2,64,64]{2,1,0:T(8,128)S(1)}, f32[2,64,64,128]{3,2,1,0:T(8,128)}, s32[]{:T(128)}, /*index=5*/...) while((s32[]{:T(128)}, f32[2,64,64]{2,1,0:T(8,128)S(1)}, ...), condition=%wide.region_6.7_spmd.clone, body=%wide.region_2.6_spmd.clone.sunk | while | flops 277900800 | bytes 48851412 | solution.py:109
  139.4 2.8 %gather_fusion = bf16[128,64,256]{2,1,0:T(8,128)(2,1)} fusion(bf16[66,64,1,256]{3,1,2,0:T(8,128)(2,1)S(1)} %get-tuple-element.738, s32[128]{0:T(128)S(1)} %reshape.570), kind=kCustom, calls=%fused_computation.clone.clone.1 | custom fusion | bytes 8389632 | tf_op jit(solution)/shard_map/while/body/gather | solution.py:72
  142.3 3.5 %fusion.73 = (f32[2,64,64]{2,1,0:T(8,128)S(1)}, f32[2,64,64,64]{3,2,1,0:T(8,128)S(1)}) fusion(pred[64,64]{0,1:T(8,128)(4,1)S(1)} %fusion.70, pred[2,64]{1,0:T(4,128)(4,1)S(1)} %and_or_fusion.2, bf16[2,64,64,128]{3,2,1,0:T(8,128)(2,1)} %get-tuple-element.739, bf16[2,64,64,256]{3,2,1,0:T(8,128)(2,1)} %bitcast.106), kind=kOutput, calls=%fused_computation.13.clone.1 | convolution fusion | flops 136306688 | bytes 6328448 | tf_op jit(solution)/shard_map/while/body/inqd,inkd->inqk/dot_general | solution.py:76
  148.1 6.1 %multiply_add_fusion.9 = f32[2,64,64,128]{3,2,1,0:T(8,128)} fusion(f32[2,64,64,128]{3,2,1,0:T(8,128)} %get-tuple-element.717, f32[2,64,64,64]{3,2,1,0:T(8,128)S(1)} %get-tuple-element.677, bf16[2,64,64,256]{3,2,1,0:T(8,128)(2,1)S(1)} %bitcast.107, f32[2,64,64]{2,1,0:T(8,128)S(1)} %get-tuple-element.679, f32[2,64,64]{2,1,0:T(8,128)S(1)} %max.42, ...), kind=kOutput, calls=%fused_computation.16.clone.1 | convolution fusion | flops 138936320 | bytes 14819840 | tf_op jit(solution)/shard_map/while/body/inqk,inkd->inqd/dot_general | solution.py:84
  157.5 3.5 %fusion.73 = (f32[2,64,64]{2,1,0:T(8,128)S(1)}, f32[2,64,64,64]{3,2,1,0:T(8,128)S(1)}) fusion(pred[64,64]{0,1:T(8,128)(4,1)S(1)} %fusion.70, pred[2,64]{1,0:T(4,128)(4,1)S(1)} %and_or_fusion.2, bf16[2,64,64,128]{3,2,1,0:T(8,128)(2,1)} %get-tuple-element.739, bf16[2,64,64,256]{3,2,1,0:T(8,128)(2,1)} %bitcast.106), kind=kOutput, calls=%fused_computation.13.clone.1 | convolution fusion | flops 136306688 | bytes 6328448 | tf_op jit(solution)/shard_map/while/body/inqd,inkd->inqk/dot_general | solution.py:76
  163.3 6.2 %multiply_add_fusion.9 = f32[2,64,64,128]{3,2,1,0:T(8,128)} fusion(f32[2,64,64,128]{3,2,1,0:T(8,128)} %get-tuple-element.717, f32[2,64,64,64]{3,2,1,0:T(8,128)S(1)} %get-tuple-element.677, bf16[2,64,64,256]{3,2,1,0:T(8,128)(2,1)S(1)} %bitcast.107, f32[2,64,64]{2,1,0:T(8,128)S(1)} %get-tuple-element.679, f32[2,64,64]{2,1,0:T(8,128)S(1)} %max.42, ...), kind=kOutput, calls=%fused_computation.16.clone.1 | convolution fusion | flops 138936320 | bytes 14819840 | tf_op jit(solution)/shard_map/while/body/inqk,inkd->inqd/dot_general | solution.py:84
  172.7 3.6 %fusion.73 = (f32[2,64,64]{2,1,0:T(8,128)S(1)}, f32[2,64,64,64]{3,2,1,0:T(8,128)S(1)}) fusion(pred[64,64]{0,1:T(8,128)(4,1)S(1)} %fusion.70, pred[2,64]{1,0:T(4,128)(4,1)S(1)} %and_or_fusion.2, bf16[2,64,64,128]{3,2,1,0:T(8,128)(2,1)} %get-tuple-element.739, bf16[2,64,64,256]{3,2,1,0:T(8,128)(2,1)} %bitcast.106), kind=kOutput, calls=%fused_computation.13.clone.1 | convolution fusion | flops 136306688 | bytes 6328448 | tf_op jit(solution)/shard_map/while/body/inqd,inkd->inqk/dot_general | solution.py:76
  178.4 6.1 %multiply_add_fusion.9 = f32[2,64,64,128]{3,2,1,0:T(8,128)} fusion(f32[2,64,64,128]{3,2,1,0:T(8,128)} %get-tuple-element.717, f32[2,64,64,64]{3,2,1,0:T(8,128)S(1)} %get-tuple-element.677, bf16[2,64,64,256]{3,2,1,0:T(8,128)(2,1)S(1)} %bitcast.107, f32[2,64,64]{2,1,0:T(8,128)S(1)} %get-tuple-element.679, f32[2,64,64]{2,1,0:T(8,128)S(1)} %max.42, ...), kind=kOutput, calls=%fused_computation.16.clone.1 | convolution fusion | flops 138936320 | bytes 14819840 | tf_op jit(solution)/shard_map/while/body/inqk,inkd->inqd/dot_general | solution.py:84
  184.6 3.1 %reduce_sum.53 = bf16[2,4,64,256]{3,2,1,0:T(8,128)(2,1)S(1)} reduce(bf16[16,2,4,64,256]{4,3,2,1,0:T(8,128)(2,1)} %bitcast.114, bf16[]{:T(256)} %constant.224.clone.1), dimensions={0}, to_apply=%region_9.10 | reduce | flops 1966080 | bytes 4456450 | tf_op jit(solution)/shard_map/reduce_sum | solution.py:15
  187.7 44.2 %while.35 = (s32[]{:T(128)}, f32[2,64,64]{2,1,0:T(8,128)S(1)}, f32[2,64,64]{2,1,0:T(8,128)S(1)}, f32[2,64,64,128]{3,2,1,0:T(8,128)}, s32[]{:T(128)}, /*index=5*/...) while((s32[]{:T(128)}, f32[2,64,64]{2,1,0:T(8,128)S(1)}, ...), condition=%wide.region_13.15_spmd.clone, body=%wide.region_10.14_spmd.clone.sunk | while | flops 276317728 | bytes 19667008 | solution.py:110
  192.6 6.0 %multiply_add_fusion.11 = f32[2,64,64,128]{3,2,1,0:T(8,128)} fusion(f32[2,64,64,128]{3,2,1,0:T(8,128)} %get-tuple-element.765, f32[2,64,64,64]{3,1,2,0:T(8,128)S(1)} %get-tuple-element.695, f32[2,64,64]{2,1,0:T(8,128)S(1)} %get-tuple-element.697, f32[2,64,64]{2,1,0:T(8,128)S(1)} %max.43, pred[2,64]{1,0:T(4,128)(4,1)S(1)} %compare_and_fusion.2, ...), kind=kOutput, calls=%fused_computation.49.clone.1 | convolution fusion | flops 138412032 | bytes 12747264 | tf_op jit(solution)/shard_map/while/body/inqk,ikd->inqd/dot_general | solution.py:104
  203.5 6.0 %multiply_add_fusion.11 = f32[2,64,64,128]{3,2,1,0:T(8,128)} fusion(f32[2,64,64,128]{3,2,1,0:T(8,128)} %get-tuple-element.765, f32[2,64,64,64]{3,1,2,0:T(8,128)S(1)} %get-tuple-element.695, f32[2,64,64]{2,1,0:T(8,128)S(1)} %get-tuple-element.697, f32[2,64,64]{2,1,0:T(8,128)S(1)} %max.43, pred[2,64]{1,0:T(4,128)(4,1)S(1)} %compare_and_fusion.2, ...), kind=kOutput, calls=%fused_computation.49.clone.1 | convolution fusion | flops 138412032 | bytes 12747264 | tf_op jit(solution)/shard_map/while/body/inqk,ikd->inqd/dot_general | solution.py:104
  214.4 6.0 %multiply_add_fusion.11 = f32[2,64,64,128]{3,2,1,0:T(8,128)} fusion(f32[2,64,64,128]{3,2,1,0:T(8,128)} %get-tuple-element.765, f32[2,64,64,64]{3,1,2,0:T(8,128)S(1)} %get-tuple-element.695, f32[2,64,64]{2,1,0:T(8,128)S(1)} %get-tuple-element.697, f32[2,64,64]{2,1,0:T(8,128)S(1)} %max.43, pred[2,64]{1,0:T(4,128)(4,1)S(1)} %compare_and_fusion.2, ...), kind=kOutput, calls=%fused_computation.49.clone.1 | convolution fusion | flops 138412032 | bytes 12747264 | tf_op jit(solution)/shard_map/while/body/inqk,ikd->inqd/dot_general | solution.py:104
  225.3 6.0 %multiply_add_fusion.11 = f32[2,64,64,128]{3,2,1,0:T(8,128)} fusion(f32[2,64,64,128]{3,2,1,0:T(8,128)} %get-tuple-element.765, f32[2,64,64,64]{3,1,2,0:T(8,128)S(1)} %get-tuple-element.695, f32[2,64,64]{2,1,0:T(8,128)S(1)} %get-tuple-element.697, f32[2,64,64]{2,1,0:T(8,128)S(1)} %max.43, pred[2,64]{1,0:T(4,128)(4,1)S(1)} %compare_and_fusion.2, ...), kind=kOutput, calls=%fused_computation.49.clone.1 | convolution fusion | flops 138412032 | bytes 12747264 | tf_op jit(solution)/shard_map/while/body/inqk,ikd->inqd/dot_general | solution.py:104
  232.0 3.8 %divide_convert_fusion = bf16[2,64,64,128]{3,2,1,0:T(8,128)(2,1)} fusion(f32[2,64,64,128]{3,2,1,0:T(8,128)} %get-tuple-element.217, f32[2,64,64]{2,1,0:T(8,128)S(1)} %get-tuple-element.218), kind=kLoop, calls=%fused_computation.72 | loop fusion | flops 2097152 | bytes 6324224 | tf_op jit(solution)/shard_map/convert_element_type | solution.py:112
  (135 shorter events, 45.2 us)
Async XLA Ops:
  11.0 63.3 %all-to-all-start = ((bf16[128,32,256]{2,0,1:T(8,128)(2,1)}), bf16[128,32,256]{2,0,1:T(8,128)(2,1)S(1)}, u32[]{:S(2)}, u32[]{:S(2)}) async-start(bf16[128,32,256]{2,0,1:T(8,128)(2,1)} %bitcast.111), calls=%async_computation | async-start | bytes 4194304 | tf_op jit(solution)/shard_map/all_to_all | solution.py:136
  36.5 44.1 %copy-start.3 = (s32[64,4]{0,1:T(4,128)S(1)}, s32[64,4]{0,1:T(4,128)}, u32[]{:S(2)}) copy-start(s32[64,4]{0,1:T(4,128)} %param.13) | copy-start | bytes 3076
  36.5 44.2 %copy-start.5 = (s32[64,2]{0,1:T(2,128)S(1)}, s32[64,2]{0,1:T(2,128)}, u32[]{:S(2)}) copy-start(s32[64,2]{0,1:T(2,128)} %param.14) | copy-start | bytes 1540
  36.5 44.3 %copy-start.4 = (s32[64]{0:T(128)S(1)}, s32[64]{0:T(128)}, u32[]{:S(2)}) copy-start(s32[64]{0:T(128)} %param.15) | copy-start | bytes 772
  74.2 59.2 %copy-start.2 = (bf16[128,32,256]{2,0,1:T(8,128)(2,1)}, bf16[128,32,256]{2,0,1:T(8,128)(2,1)S(1)}, u32[]{:S(2)}) copy-start(bf16[128,32,256]{2,0,1:T(8,128)(2,1)S(1)} %all-to-all-done) | copy-start | bytes 6291460
  74.2 56.0 %all-to-all-start.1 = ((bf16[2,32,128,128]{3,2,0,1:T(8,128)(2,1)}), bf16[2,32,128,128]{3,2,0,1:T(8,128)(2,1)}, u32[]{:S(2)}, u32[]{:S(2)}) async-start(bf16[2,32,128,128]{3,2,0,1:T(8,128)(2,1)} %copy.71), calls=%async_computation.1 | async-start | bytes 4194304 | tf_op jit(solution)/shard_map/all_to_all | solution.py:133
  80.6 104.0 %all-gather.3.cloned.1.call-start = ((), (), s32[]{:S(2)}) async-start(), calls=%async_computation.2 | async-start | bytes 4456448 | tf_op jit(solution)/shard_map/all_gather | solution.py:15
  84.7 48.7 %collective-permute-start = (bf16[128,256]{1,0:T(8,128)(2,1)S(1)}, bf16[128,256]{1,0:T(8,128)(2,1)S(1)}, u32[]{:S(2)}, u32[]{:S(2)}) collective-permute-start(bf16[128,256]{1,0:T(8,128)(2,1)S(1)} %slice_bitcast_fusion.4), channel_id=1, source_target_pairs={{0,32},{32,64},{64,96},{96,128},{128,160},{160,192},{192,224},{224... | collective-permute-start | bytes 196616 | tf_op jit(solution)/shard_map/ppermute | solution.py:21
  145.7 2.4 copy-start
  161.0 2.3 copy-start
  176.2 2.2 copy-start
  184.6 3.2 %copy-start.1 = (bf16[2,64,64,128]{3,2,1,0:T(8,128)(2,1)S(1)}, bf16[2,64,64,128]{3,2,1,0:T(8,128)(2,1)}, u32[]{:S(2)}) copy-start(bf16[2,64,64,128]{3,2,1,0:T(8,128)(2,1)} %get-tuple-element.795) | copy-start | bytes 6291460
Sparse Core Ops, SparseCore 0:
  136.6 41.5 all-gather.2
